TPU v7x, 32 devices: a whole 2x2x4 slice. The times are simulated.
32 devices in a mesh: seq: 8 (over y, x, core), head: 4 (over z).
Axes of the slice: x: 2, y: 2, z: 4, core: 2. Of those that a mesh axis runs over, the one named last changes fastest.
Arguments:
- activations: bfloat16 [4096, 5376], P(('seq', 'head')), may hold values from -42 to 42, as said below
- input_gain: float32 [5376], replicated, may hold values from 0.1 to 1.9
- query_weight: bfloat16 [5376, 4096], P(None, 'head'), may hold values from -2.2818633 to 2.2818633
- key_weight: bfloat16 [5376, 2048], P(None, 'head'), may hold values from -1 to 1
- value_weight: bfloat16 [5376, 2048], P(None, 'head'), may hold values from -0.078125 to 0.078125
- output_weight: bfloat16 [4096, 5376], P('head'), may hold values from -0.09375 to 0.09375
- cache_edge: bfloat16 [2, 1024, 2048], P(None, None, 'head'), may hold values from -6 to 6
- post_gain: float32 [5376], replicated, may hold values from 0.1 to 1.9
Outputs:
- layer_out: bfloat16 [4096, 5376], P(('seq', 'head'))
Inputs may be any that keep to these rules, and one draw needn't show every extreme that they name: `activations`: input rows with row and feature scales.
All inputs are finite; a program needn't handle non-finite values.
Results may differ from a plain program's by a relative error of at most 0.006.
Values may be sent and summed in bfloat16 or wider, within the bound.
A program may use at most 128 MiB of HBM per device.

v0:
```python
import functools
import jax
import jax.numpy as jnp
from jax import lax
from jax.experimental import pallas as pl
from jax.experimental.pallas import tpu as pltpu
from jax.sharding import PartitionSpec as P

HD = 128
WINDOW = 1024
SCALAR = 168
TOK_DEV = 512
EPSILON = 1e-06
ROPE_BASE = 10000.0
REACH = WINDOW // TOK_DEV
COL_CHUNKS = 7
MESH = pl.DeviceIdType.MESH


def rope_tables(positions):
    half_size = HD // 2
    frequency = ROPE_BASE ** (-(jnp.arange(half_size, dtype=jnp.float32) * 2.0 / HD))
    angles = positions[:, None] * frequency[None, :]
    cosine = jnp.cos(angles)
    sine = jnp.sin(angles)
    return jnp.concatenate([cosine, cosine], axis=1), jnp.concatenate([-sine, sine], axis=1)


def kernel(
    n, s_count,
    act_ref, gain_ref, wq_hbm, wk_hbm, wv_hbm, wo_hbm, cache_hbm, post_ref, cos_ref, sin_ref,
    out_ref,
    wq, wk, wv, wo, rows, q_buf, kv, att, slots, acc,
    w_sem, cache_sem, ag_send, ag_recv, kv_send, kv_recv, rs_send, rs_recv,
):
    s = lax.axis_index("seq")
    z = lax.axis_index("head")
    R, D = act_ref.shape
    kv_width = wk.shape[1]
    heads_kv = kv_width // HD
    group = wq.shape[1] // kv_width
    row_chunks = ag_send.shape[2]
    CR = R // row_chunks
    CD = D // COL_CHUNKS

    weight_copies = [
        pltpu.make_async_copy(src, dst, w_sem.at[i])
        for i, (src, dst) in enumerate([(wk_hbm, wk), (wv_hbm, wv), (wq_hbm, wq), (wo_hbm, wo)])
    ]
    for c in weight_copies:
        c.start()

    def cache_copies(d):
        return [
            pltpu.make_async_copy(
                cache_hbm.at[i, pl.ds(pl.multiple_of(WINDOW + (s - d) * TOK_DEV, TOK_DEV), TOK_DEV), :],
                kv.at[pl.ds(WINDOW - d * TOK_DEV, TOK_DEV), pl.ds(i * kv_width, kv_width)],
                cache_sem.at[d - 1, i],
            )
            for i in range(2)
        ]

    for d in range(1, REACH + 1):
        @pl.when(s < d)
        def _():
            for c in cache_copies(d):
                c.start()

    barrier = pltpu.get_barrier_semaphore()

    def greet(cond, ds, dz):
        @pl.when(cond)
        def _():
            pl.semaphore_signal(barrier, inc=1, device_id=(s + ds, z + dz), device_id_type=MESH)

    partners = [(z > 0, 0, -1), (z < n - 1, 0, 1)]
    for d in range(1, REACH + 1):
        partners += [(s >= d, -d, 0), (s + d < s_count, d, 0)]
    for p in partners:
        greet(*p)

    def norm_chunk(i, carry):
        r0 = pl.multiple_of(i * 16, 16)
        x = act_ref[pl.ds(r0, 16), :].astype(jnp.float32)
        y = x * lax.rsqrt(jnp.mean(x * x, axis=-1, keepdims=True) + EPSILON) * gain_ref[...].reshape(1, D)
        rows[z, pl.ds(r0, 16), :] = y.astype(jnp.bfloat16)
        return carry

    pl.semaphore_wait(barrier, sum(jnp.where(p[0], 1, 0) for p in partners))

    right = lax.rem(z + 1, n)
    left = lax.rem(z + n - 1, n)

    def ag_copy(direction, block, c):
        where = rows.at[block, pl.ds(c * CR, CR), :]
        return pltpu.make_async_remote_copy(
            src_ref=where, dst_ref=where,
            send_sem=ag_send.at[direction, block, c], recv_sem=ag_recv.at[direction, block, c],
            device_id=(s, right if direction == 0 else left), device_id_type=MESH,
        )

    def kv_copy(d, block):
        r0 = pl.multiple_of(block * R, R)
        return pltpu.make_async_remote_copy(
            src_ref=kv.at[pl.ds(WINDOW + r0, R), :],
            dst_ref=kv.at[pl.ds(WINDOW - d * TOK_DEV + r0, R), :],
            send_sem=kv_send.at[d - 1, block], recv_sem=kv_recv.at[d - 1, block],
            device_id=(lax.rem(s + d, s_count), z), device_id_type=MESH,
        )

    def rs_copy(direction, block, slot, c):
        where = slots.at[slot, c]
        return pltpu.make_async_remote_copy(
            src_ref=where, dst_ref=where,
            send_sem=rs_send.at[direction, block, c], recv_sem=rs_recv.at[direction, block, c],
            device_id=(s, right if direction == 0 else left), device_id_type=MESH,
        )

    def project(block):
        r0 = pl.multiple_of(block * R, R)
        cosine = cos_ref[pl.ds(r0, R), :]
        sine = sin_ref[pl.ds(r0, R), :]

        def run(w, tile, rotary, scale, dst, dst_r0, dst_c0):
            def one(i, carry):
                c0 = pl.multiple_of(i * tile, tile)
                t = jnp.dot(rows[block], w[:, pl.ds(c0, tile)], preferred_element_type=jnp.float32)
                for h in range(tile // HD):
                    u = t[:, h * HD:(h + 1) * HD]
                    if rotary:
                        u = u * cosine + pltpu.roll(u, HD // 2, 1) * sine
                    if scale is not None:
                        u = u * scale
                    dst[pl.ds(dst_r0, R), pl.ds(pl.multiple_of(dst_c0 + c0 + h * HD, HD), HD)] = u.astype(jnp.bfloat16)
                return carry
            lax.fori_loop(0, w.shape[1] // tile, one, 0)

        tile = min(256, kv_width)
        own = pl.multiple_of(WINDOW + r0, R)
        run(wk, tile, True, None, kv, own, 0)
        run(wv, tile, False, None, kv, own, kv_width)
        for d in range(1, REACH + 1):
            @pl.when(s + d < s_count)
            def _():
                kv_copy(d, block).start()
        run(wq, 256, True, SCALAR ** (-0.5), q_buf, r0, 0)

    for c in range(row_chunks):
        lax.fori_loop(c * CR // 16, (c + 1) * CR // 16, norm_chunk, 0)

        @pl.when(z < n - 1)
        def _():
            ag_copy(0, z, c).start()

        @pl.when(z > 0)
        def _():
            ag_copy(1, z, c).start()

    for i in range(3):
        weight_copies[i].wait()
    def gather_step(t, carry):
        from_left = z - t
        from_right = z + t
        for c in range(row_chunks):
            @pl.when(from_left >= 0)
            def _():
                ag_copy(0, from_left, c).wait_recv()

                @pl.when(z < n - 1)
                def _():
                    ag_copy(0, from_left, c).start()

            @pl.when(from_right < n)
            def _():
                ag_copy(1, from_right, c).wait_recv()

                @pl.when(z > 0)
                def _():
                    ag_copy(1, from_right, c).start()

            if c == 0:
                @pl.when(from_right - 1 < n)
                def _():
                    project(from_right - 1)

        @pl.when(from_left >= 0)
        def _():
            project(from_left)
        return carry

    lax.fori_loop(1, n, gather_step, 0)

    @pl.when(z == 0)
    def _():
        project(n - 1)

    for d in range(1, REACH + 1):
        @pl.when(s < d)
        def _():
            for c in cache_copies(d):
                c.wait()

        @pl.when(s >= d)
        def _():
            lax.fori_loop(0, n, lambda b, carry: (kv_copy(d, b).wait_recv(), carry)[1], 0)
    weight_copies[3].wait()

    row_i = lax.broadcasted_iota(jnp.int32, (group * R, R), 0)
    row_i = lax.rem(row_i, R)
    col_i = lax.broadcasted_iota(jnp.int32, (group * R, R), 1)
    later = col_i > row_i
    spans = [(0, R), (R, WINDOW - R), (WINDOW, R)]

    def attend(block):
        r0 = pl.multiple_of(block * R, R)
        for g in range(heads_kv):
            q = jnp.concatenate(
                [q_buf[pl.ds(r0, R), (g * group + a) * HD:(g * group + a + 1) * HD] for a in range(group)], axis=0
            )
            scores = []
            for j, (o, w) in enumerate(spans):
                k = kv[pl.ds(pl.multiple_of(r0 + o, R), w), g * HD:(g + 1) * HD]
                sc = lax.dot_general(q, k, (((1,), (1,)), ((), ())), preferred_element_type=jnp.float32)
                if j == 0:
                    sc = jnp.where(later, sc, -jnp.inf)
                if j == 2:
                    sc = jnp.where(later, -jnp.inf, sc)
                scores.append(sc)
            m = functools.reduce(jnp.maximum, [jnp.max(x, axis=-1, keepdims=True) for x in scores])
            total = 0.0
            o_sum = 0.0
            for (o, w), sc in zip(spans, scores):
                e = jnp.exp(sc - m)
                total = total + jnp.sum(e, axis=-1, keepdims=True)
                v = kv[pl.ds(pl.multiple_of(r0 + o, R), w), kv_width + g * HD:kv_width + (g + 1) * HD]
                o_sum = o_sum + jnp.dot(e.astype(jnp.bfloat16), v, preferred_element_type=jnp.float32)
            o_sum = (o_sum / total).astype(jnp.bfloat16)
            for a in range(group):
                att[:, (g * group + a) * HD:(g * group + a + 1) * HD] = o_sum[a * R:(a + 1) * R]

    TILE = 256

    def partial_out(direction, block, incoming):
        attend(block)
        for c in range(COL_CHUNKS):
            @pl.when(incoming)
            def _():
                rs_copy(direction, block, block, c).wait_recv()

            def one(i, carry):
                c0 = pl.multiple_of(i * TILE, TILE)
                w0 = pl.multiple_of(c * CD + i * TILE, TILE)
                p = jnp.dot(att[...], wo[:, pl.ds(w0, TILE)], preferred_element_type=jnp.float32)
                before = slots[block, c, :, pl.ds(c0, TILE)].astype(jnp.float32)
                p = p + jnp.where(incoming, before, 0.0)
                slots[block, c, :, pl.ds(c0, TILE)] = p.astype(jnp.bfloat16)
                return carry
            lax.fori_loop(0, CD // TILE, one, 0)
            send_out(direction, block, c).start()

    def send_out(direction, block, c):
        if direction == 0:
            return rs_copy(0, block, block, c)
        last = jnp.where(block == z - 1, n, block)
        return pltpu.make_async_remote_copy(
            src_ref=slots.at[block, c], dst_ref=slots.at[last, c],
            send_sem=rs_send.at[1, block, c], recv_sem=rs_recv.at[1, block, c],
            device_id=(s, left), device_id_type=MESH,
        )

    def scatter_step(t, carry):
        to_right = n - t
        to_left = t - 1

        @pl.when(to_right > z)
        def _():
            partial_out(0, to_right, z > 0)

        @pl.when(to_left < z)
        def _():
            partial_out(1, to_left, z < n - 1)
        return carry

    lax.fori_loop(1, n, scatter_step, 0)

    attend(z)

    def own(i, carry):
        w0 = pl.multiple_of(i * TILE, TILE)
        acc[:, pl.ds(w0, TILE)] = jnp.dot(att[...], wo[:, pl.ds(w0, TILE)], preferred_element_type=jnp.float32)
        return carry
    lax.fori_loop(0, D // TILE, own, 0)

    for c in range(COL_CHUNKS):
        for direction, slot, cond in ((0, z, z > 0), (1, n, z < n - 1)):
            @pl.when(cond)
            def _():
                rs_copy(direction, z, slot, c).wait_recv()
                acc[:, c * CD:(c + 1) * CD] += slots[slot, c].astype(jnp.float32)

    def finish(i, carry):
        r0 = pl.multiple_of(i * 16, 16)
        x = acc[pl.ds(r0, 16), :]
        y = x * lax.rsqrt(jnp.mean(x * x, axis=-1, keepdims=True) + EPSILON) * post_ref[...].reshape(1, D)
        out_ref[pl.ds(r0, 16), :] = (act_ref[pl.ds(r0, 16), :].astype(jnp.float32) + y).astype(jnp.bfloat16)
        return carry
    lax.fori_loop(0, R // 16, finish, 0)

    def drain(b, carry):
        @pl.when((b <= z) & (z < n - 1))
        def _():
            for c in range(row_chunks):
                ag_copy(0, b, c).wait_send()

        @pl.when((b >= z) & (z > 0))
        def _():
            for c in range(row_chunks):
                ag_copy(1, b, c).wait_send()

        @pl.when(b > z)
        def _():
            for c in range(COL_CHUNKS):
                send_out(0, b, c).wait_send()

        @pl.when(b < z)
        def _():
            for c in range(COL_CHUNKS):
                send_out(1, b, c).wait_send()

        for d in range(1, REACH + 1):
            @pl.when(s + d < s_count)
            def _():
                kv_copy(d, b).wait_send()
        return carry
    lax.fori_loop(0, n, drain, 0)


def per_device(n, s_count, act, gain, wq, wk, wv, wo, cache, post):
    R, D = act.shape
    row_chunks = min(4, R // 16)
    s = lax.axis_index("seq")
    positions = (s * TOK_DEV + jnp.arange(TOK_DEV, dtype=jnp.int32)).astype(jnp.float32)
    cosine, sine = rope_tables(positions)
    bf, f32 = jnp.bfloat16, jnp.float32
    vmem = pl.BlockSpec(memory_space=pltpu.VMEM)
    hbm = pl.BlockSpec(memory_space=pl.ANY)
    dma = pltpu.SemaphoreType.DMA
    return pl.pallas_call(
        functools.partial(kernel, n, s_count),
        out_shape=jax.ShapeDtypeStruct((R, D), bf),
        in_specs=[vmem, vmem, hbm, hbm, hbm, hbm, hbm, vmem, vmem, vmem],
        out_specs=vmem,
        scratch_shapes=[
            pltpu.VMEM(wq.shape, bf),
            pltpu.VMEM(wk.shape, bf),
            pltpu.VMEM(wv.shape, bf),
            pltpu.VMEM(wo.shape, bf),
            pltpu.VMEM((n, R, D), bf),
            pltpu.VMEM((TOK_DEV, wq.shape[1]), bf),
            pltpu.VMEM((WINDOW + TOK_DEV, 2 * wk.shape[1]), bf),
            pltpu.VMEM((R, wo.shape[0]), bf),
            pltpu.VMEM((n + 1, COL_CHUNKS, R, D // COL_CHUNKS), bf),
            pltpu.VMEM((R, D), f32),
            dma((4,)),
            dma((REACH, 2)),
            dma((2, n, row_chunks)),
            dma((2, n, row_chunks)),
            dma((REACH, n)),
            dma((REACH, n)),
            dma((2, n, COL_CHUNKS)),
            dma((2, n, COL_CHUNKS)),
        ],
        compiler_params=pltpu.CompilerParams(
            collective_id=0, has_side_effects=True, vmem_limit_bytes=62 * 1024 * 1024
        ),
    )(act, gain, wq, wk, wv, wo, cache, post, cosine, sine)


def solution(mesh):
    return jax.shard_map(
        functools.partial(per_device, mesh.shape["head"], mesh.shape["seq"]),
        mesh=mesh,
        in_specs=(
            P(("seq", "head"), None),
            P(),
            P(None, "head"),
            P(None, "head"),
            P(None, "head"),
            P("head", None),
            P(None, None, "head"),
            P(),
        ),
        out_specs=P(("seq", "head"), None),
        check_vma=False,
    )
```

profile of v0, /device:TPU:20, one launch (start us, length us, event | category | flops | bytes accessed | tf_op | source)
XLA Modules:
  0.0 226.0 jit_solution(9304072331442685138)
XLA Ops:
  0.0 1.0 fusion
  1.0 1.0 pad_maximum_fusion
  2.0 221.5 %shard_map.82 = bf16[128,5376]{1,0:T(8,128)(2,1)} custom-call(bf16[128,5376]{1,0:T(8,128)(2,1)} %act_ref.1, f32[5376]{0:T(1024)} %gain_ref.1, bf16[5376,1024]{1,0:T(8,128)(2,1)} %wq_hbm.1, bf16[5376,512]{1,0:T(8,128)(2,1)} %wk_hbm.1, bf16[5376,512]{1,0:T(8,128)(2,1)} %wv_hbm.1, bf16[1024,5376]{1,0:T(8,128)(2,1)} %wo_hbm.1, bf16[2,1024,512]{2,1,0:T(8,128)(2,1)} %cache_hbm.1, ...), custom_call_target="tpu_custom_call" | custom-call | tf_op jit(solution)/shard_map/pallas_call | solution.py:348
  223.5 2.5 %copy.10 = bf16[128,5376]{1,0:T(8,128)(2,1)} copy(bf16[128,5376]{1,0:T(8,128)(2,1)} %shard_map.82) | data formatting | bytes 2752512
  (2 shorter events, 0.0 us)
where the time goes:
time: 226 us
  Pallas kernels  221 us (98%)
  local copies, waits for them, and re-layouts  2.51 us (1%)
    pallas_call x1, Pallas kernels, per_device(): pl.pallas_call(functools.partial(kernel, n, s_count), out_shape=jax.Shape...  221 us

commit v1 on v0

--- a/solution.py
+++ b/solution.py
@@ -376,9 +376,493 @@
     )(act, gain, wq, wk, wv, wo, cache, post, cosine, sine)
 
 
+PHASES = 4
+CHIPS = 4
+CORES = 2
+
+
+def phased_kernel(
+    act_ref, gain_ref, wq_hbm, wk_hbm, wv_hbm, wo_hbm, cache_hbm, post_ref, cos_ref, sin_ref,
+    out_ref,
+    w, wo, act_in, rows, q_buf, kv, att, att_x, slots, acc, stage,
+    w_sem, cache_sem, spread_send, spread_recv, ag_send, ag_recv, core_send, core_recv,
+    kv_send, kv_recv, att_send, att_recv, rs_send, rs_recv, out_send, out_recv,
+):
+    n = 4
+    s = lax.axis_index("seq")
+    z = lax.axis_index("head")
+    c = s // CORES
+    k = lax.rem(s, CORES)
+    B, D = act_in.shape[1:]
+    KW = wk_hbm.shape[1] // CORES
+    QW = wq_hbm.shape[1] // CORES
+    heads_kv = KW // HD
+    group = QW // KW
+    bf, f32 = jnp.bfloat16, jnp.float32
+    near = z // 2
+    inner = (z > 0) & (z < n - 1)
+    outer = (z == 0) | (z == n - 1)
+
+    def remote(src, dst, send, recv, chip, core, plane):
+        return pltpu.make_async_remote_copy(
+            src_ref=src, dst_ref=dst, send_sem=send, recv_sem=recv,
+            device_id=(chip * CORES + core, plane), device_id_type=MESH,
+        )
+
+    def chip_at(d):
+        return [c + 1 - 2 * lax.rem(c, 2), lax.rem(c + 2, CHIPS), CHIPS - 1 - c][d]
+
+    weight_copies = [
+        pltpu.make_async_copy(wk_hbm.at[:, pl.ds(pl.multiple_of(k * KW, KW), KW)], w.at[:, pl.ds(0, KW)], w_sem.at[0]),
+        pltpu.make_async_copy(wv_hbm.at[:, pl.ds(pl.multiple_of(k * KW, KW), KW)], w.at[:, pl.ds(KW, KW)], w_sem.at[1]),
+        pltpu.make_async_copy(wq_hbm.at[:, pl.ds(pl.multiple_of(k * QW, QW), QW)], w.at[:, pl.ds(2 * KW, QW)], w_sem.at[2]),
+        pltpu.make_async_copy(wo_hbm, wo, w_sem.at[3]),
+    ]
+    cache_copies = [
+        pltpu.make_async_copy(
+            cache_hbm.at[i, :, :, :, :, pl.ds(pl.multiple_of(k * KW, KW), KW)],
+            kv.at[pl.ds(0, 4), :, :, :, pl.ds(i * KW, KW)],
+            cache_sem.at[i],
+        )
+        for i in range(2)
+    ]
+
+    barrier = pltpu.get_barrier_semaphore()
+
+    def greet(chip, core, plane):
+        pl.semaphore_signal(barrier, inc=1, device_id=(chip * CORES + core, plane), device_id_type=MESH)
+
+    for d in range(3):
+        greet(chip_at(d), k, z)
+    greet(c, 1 - k, z)
+
+    @pl.when(z > 0)
+    def _():
+        greet(c, k, z - 1)
+
+    @pl.when(z < n - 1)
+    def _():
+        greet(c, k, z + 1)
+
+    for x in weight_copies + cache_copies:
+        x.start()
+    pl.semaphore_wait(barrier, 4 + jnp.where(inner, 2, 1))
+
+    def spread_copy(d):
+        to = chip_at(d)
+        return remote(
+            act_ref.at[pl.ds(pl.multiple_of(to * B, B), B), :], act_in.at[c],
+            spread_send.at[d], spread_recv.at[c], to, k, z,
+        )
+
+    def spread_wait(t):
+        remote(act_in.at[t], act_in.at[t], spread_send.at[0], spread_recv.at[t], c, k, z).wait_recv()
+
+    def row_block(t, core, zb):
+        return rows.at[t, zb // 2, core, lax.rem(zb, 2)]
+
+    def ag_copy(t, direction, zb):
+        where = row_block(t, k, zb)
+        to = jnp.minimum(z + 1, n - 1) if direction == 0 else jnp.maximum(z - 1, 0)
+        return remote(where, where, ag_send.at[t, direction, zb], ag_recv.at[t, zb], c, k, to)
+
+    def core_copy(t, zb, core):
+        where = row_block(t, core, zb)
+        return remote(where, where, core_send.at[t, zb], core_recv.at[t, zb], c, 1 - k, z)
+
+    def normalize(t):
+        @pl.when(t != c)
+        def _():
+            spread_wait(t)
+
+        def piece(i, carry):
+            r0 = pl.multiple_of(i * 16, 16)
+            x = act_in[t, pl.ds(r0, 16), :].astype(f32)
+            y = x * lax.rsqrt(jnp.mean(x * x, axis=-1, keepdims=True) + EPSILON) * gain_ref[...].reshape(1, D)
+            rows[t, near, k, lax.rem(z, 2), pl.ds(r0, 16), :] = y.astype(bf)
+            return carry
+        lax.fori_loop(0, B // 16, piece, 0)
+
+    def forward(t, zb, right, left):
+        if right:
+            @pl.when(z < n - 1)
+            def _():
+                ag_copy(t, 0, zb).start()
+        if left:
+            @pl.when(z > 0)
+            def _():
+                ag_copy(t, 1, zb).start()
+        core_copy(t, zb, k).start()
+
+    def hop(t, h):
+        @pl.when(z - h >= 0)
+        def _():
+            ag_copy(t, 0, z - h).wait_recv()
+            forward(t, z - h, True, False)
+
+        @pl.when(z + h < n)
+        def _():
+            ag_copy(t, 1, z + h).wait_recv()
+            forward(t, z + h, False, True)
+
+    def kv_copy(t, half, core, d, chip):
+        where = kv.at[4 + 2 * (2 * t + core) + half, :, chip]
+        return remote(where, where, kv_send.at[t, half, core, d], kv_recv.at[t, half, core, d], chip_at(d), k, z)
+
+    def project(t, half):
+        for i in range(2):
+            core_copy(t, 2 * half + i, 1 - k).wait_recv()
+        cosine = cos_ref[t, half]
+        sine = sin_ref[t, half]
+        x = rows.at[t, half]
+
+        def matmul(c0, width):
+            return jnp.dot(
+                x[...].reshape(4 * B, D), w[:, pl.ds(c0, width)], preferred_element_type=f32
+            )
+
+        def rope(u):
+            return u * cosine + pltpu.roll(u, HD // 2, 1) * sine
+
+        for part in range(2):
+            u = matmul(part * KW, KW)
+            for h in range(heads_kv):
+                v = u[:, h * HD:(h + 1) * HD]
+                v = (rope(v) if part == 0 else v).astype(bf)
+                for core in range(2):
+                    for zz in range(2):
+                        r0 = (core * 2 + zz) * B
+                        c0 = part * KW + h * HD
+                        kv[4 + 2 * (2 * t + core) + half, zz, c, :, c0:c0 + HD] = v[r0:r0 + B]
+        for d in range(3):
+            for core in range(2):
+                kv_copy(t, half, core, 2 - d, c).start()
+
+        def queries(i, carry):
+            c0 = pl.multiple_of(i * 256, 256)
+            u = matmul(2 * KW + c0, 256)
+            for h in range(256 // HD):
+                v = (rope(u[:, h * HD:(h + 1) * HD]) * SCALAR ** (-0.5)).astype(bf)
+                for core in range(2):
+                    q_buf[t, half, core, :, pl.ds(pl.multiple_of(c0 + h * HD, HD), HD)] = v[core * 2 * B:(core + 1) * 2 * B]
+            return carry
+        lax.fori_loop(0, QW // 256, queries, 0)
+
+    M = group * 2 * B
+    row = lax.rem(lax.broadcasted_iota(jnp.int32, (M, 256), 0), 2 * B)
+    place = (row // B) * (CHIPS * B) + lax.rem(row, B) + c * B
+    later = lax.broadcasted_iota(jnp.int32, (M, 256), 1) > place
+    spans = [(0, 1), (1, 3), (4, 1)]
+
+    def attend(t, core, half, dst, dst_c0):
+        u = 2 * (2 * t + core) + half
+        for g in range(heads_kv):
+            q = jnp.concatenate(
+                [q_buf[t, half, core, :, (g * group + a) * HD:(g * group + a + 1) * HD] for a in range(group)], axis=0
+            )
+            scores = []
+            for j, (o, wd) in enumerate(spans):
+                key = kv[pl.ds(u + o, wd), :, :, :, g * HD:(g + 1) * HD].reshape(wd * 256, HD)
+                sc = lax.dot_general(q, key, (((1,), (1,)), ((), ())), preferred_element_type=f32)
+                if j == 0:
+                    sc = jnp.where(later, sc, -jnp.inf)
+                if j == 2:
+                    sc = jnp.where(later, -jnp.inf, sc)
+                scores.append(sc)
+            m = functools.reduce(jnp.maximum, [jnp.max(x, axis=-1, keepdims=True) for x in scores])
+            total = 0.0
+            o_sum = 0.0
+            for (o, wd), sc in zip(spans, scores):
+                e = jnp.exp(sc - m)
+                total = total + jnp.sum(e, axis=-1, keepdims=True)
+                v = kv[pl.ds(u + o, wd), :, :, :, KW + g * HD:KW + (g + 1) * HD].reshape(wd * 256, HD)
+                o_sum = o_sum + jnp.dot(e.astype(bf), v, preferred_element_type=f32)
+            o_sum = (o_sum / total).astype(bf)
+            for a in range(group):
+                c0 = dst_c0 + (g * group + a) * HD
+                dst[t, half, :, pl.ds(pl.multiple_of(c0, HD), HD)] = o_sum[a * 2 * B:(a + 1) * 2 * B]
+
+    def attend_halves(t, core, dst, dst_c0):
+        def one(half, carry):
+            attend(t, core, half, dst, dst_c0)
+            return carry
+        lax.fori_loop(0, 2, one, 0)
+
+    def att_copy(t, core):
+        return remote(
+            att_x.at[t], att.at[t, :, :, pl.ds(pl.multiple_of(core * QW, QW), QW)],
+            att_send.at[t], att_recv.at[t], c, 1 - k, z,
+        )
+
+    TILE = 256
+
+    def project_out(t):
+        def one(i, carry):
+            w0 = pl.multiple_of(i * TILE, TILE)
+            p = jnp.dot(att[t].reshape(n * B, CORES * QW), wo[:, pl.ds(w0, TILE)], preferred_element_type=f32)
+            acc[lax.rem(t, 2), :, :, pl.ds(w0, TILE)] = p.reshape(n, B, TILE)
+            return carry
+        lax.fori_loop(0, D // TILE, one, 0)
+
+    def relay_block(r):
+        low = z < 2
+        if r == 0:
+            return jnp.where(low, n - 1, 0)
+        if r == 1:
+            return jnp.where(low, n - 2, 1)
+        return z + 1 - 2 * lax.rem(z, 2)
+
+    def rs_copy(t, b):
+        up = b > z
+        to = jnp.where(up, z + 1, z - 1)
+        slot = jnp.where(b == z - 1, n, b)
+        return remote(slots.at[t, b], slots.at[t, slot], rs_send.at[t, b], rs_recv.at[t, slot], c, k, to)
+
+    def rs_wait(t, slot):
+        remote(slots.at[t, slot], slots.at[t, slot], rs_send.at[t, 0], rs_recv.at[t, slot], c, k, z).wait_recv()
+
+    WIDE = 768
+
+    def relay(t, r, incoming):
+        b = relay_block(r)
+        if incoming:
+            rs_wait(t, b)
+
+        def one(i, carry):
+            c0 = pl.multiple_of(i * WIDE, WIDE)
+            x = acc[lax.rem(t, 2), b, :, pl.ds(c0, WIDE)]
+            if incoming:
+                x = x + slots[t, b, :, pl.ds(c0, WIDE)].astype(f32)
+            slots[t, b, :, pl.ds(c0, WIDE)] = x.astype(bf)
+            return carry
+        lax.fori_loop(0, D // WIDE, one, 0)
+        rs_copy(t, b).start()
+
+    def out_copy(t):
+        return remote(
+            stage.at[t], out_ref.at[pl.ds(pl.multiple_of(c * B, B), B), :], out_send.at[t], out_recv.at[c], t, k, z,
+        )
+
+    def finish(t):
+        @pl.when(z > 0)
+        def _():
+            rs_wait(t, z)
+
+        @pl.when(z < n - 1)
+        def _():
+            rs_wait(t, n)
+
+        def piece(i, carry):
+            r0 = pl.multiple_of(i * 16, 16)
+            x = acc[lax.rem(t, 2), z, pl.ds(r0, 16), :]
+            x = x + jnp.where(z > 0, slots[t, z, pl.ds(r0, 16), :].astype(f32), 0.0)
+            x = x + jnp.where(z < n - 1, slots[t, n, pl.ds(r0, 16), :].astype(f32), 0.0)
+            y = x * lax.rsqrt(jnp.mean(x * x, axis=-1, keepdims=True) + EPSILON) * post_ref[...].reshape(1, D)
+            y = (act_in[t, pl.ds(r0, 16), :].astype(f32) + y).astype(bf)
+
+            @pl.when(t == c)
+            def _():
+                out_ref[pl.ds(pl.multiple_of(c * B + r0, 16), 16), :] = y
+
+            @pl.when(t != c)
+            def _():
+                stage[t, pl.ds(r0, 16), :] = y
+            return carry
+        lax.fori_loop(0, B // 16, piece, 0)
+
+        @pl.when(t != c)
+        def _():
+            out_copy(t).start()
+
+    def spread():
+        for d in range(3):
+            spread_copy(2 - d).start()
+
+    @pl.when(c == 0)
+    def _():
+        spread()
+
+    act_in[c] = act_ref[pl.ds(pl.multiple_of(c * B, B), B), :]
+    normalize(0)
+    forward(0, z, True, True)
+
+    @pl.when(c != 0)
+    def _():
+        spread()
+
+    for x in cache_copies + weight_copies:
+        x.wait()
+
+    def slot_step(t, carry):
+        gathers = t < PHASES
+        computes = (t >= 1) & (t <= PHASES)
+        sums = t >= 2
+
+        @pl.when(gathers)
+        def _():
+            hop(t, 1)
+
+        @pl.when(computes)
+        def _():
+            project(t - 1, 1 - near)
+
+        @pl.when(t + 1 < PHASES)
+        def _():
+            normalize(t + 1)
+            forward(t + 1, z, True, True)
+
+        @pl.when(gathers)
+        def _():
+            project(t, near)
+
+        @pl.when(sums & inner)
+        def _():
+            relay(t - 2, 0, True)
+
+        @pl.when(gathers)
+        def _():
+            hop(t, 2)
+
+        @pl.when(computes)
+        def _():
+            for half in range(2):
+                for core in range(2):
+                    for d in range(3):
+                        kv_copy(t - 1, half, core, d, chip_at(d)).wait_recv()
+            attend_halves(t - 1, 1 - k, att_x, 0)
+            att_copy(t - 1, k).start()
+
+        @pl.when(sums & inner)
+        def _():
+            relay(t - 2, 1, True)
+
+        @pl.when(computes)
+        def _():
+            attend_halves(t - 1, k, att, k * QW)
+            att_copy(t - 1, 1 - k).wait_recv()
+            project_out(t - 1)
+
+            @pl.when(outer)
+            def _():
+                for r in range(3):
+                    relay(t - 1, r, False)
+
+        @pl.when(sums & inner)
+        def _():
+            relay(t - 2, 2, True)
+
+        @pl.when(sums)
+        def _():
+            finish(t - 2)
+
+        @pl.when(gathers)
+        def _():
+            hop(t, 3)
+        return carry
+
+    lax.fori_loop(0, PHASES + 2, slot_step, 0)
+
+    for d in range(3):
+        chip = chip_at(d)
+        where = out_ref.at[pl.ds(pl.multiple_of(chip * B, B), B), :]
+        remote(where, where, out_send.at[0], out_recv.at[chip], c, k, z).wait_recv()
+
+    for d in range(3):
+        spread_copy(d).wait_send()
+
+    def drain(t, carry):
+        def blocks(b, carry):
+            @pl.when((b <= z) & (z < n - 1))
+            def _():
+                ag_copy(t, 0, b).wait_send()
+
+            @pl.when((b >= z) & (z > 0))
+            def _():
+                ag_copy(t, 1, b).wait_send()
+
+            core_copy(t, b, k).wait_send()
+
+            @pl.when(b != z)
+            def _():
+                rs_copy(t, b).wait_send()
+            return carry
+        lax.fori_loop(0, n, blocks, 0)
+        for half in range(2):
+            for core in range(2):
+                for d in range(3):
+                    kv_copy(t, half, core, d, c).wait_send()
+        att_copy(t, k).wait_send()
+
+        @pl.when(t != c)
+        def _():
+            out_copy(t).wait_send()
+        return carry
+    lax.fori_loop(0, PHASES, drain, 0)
+
+
+def phased_per_device(act, gain, wq, wk, wv, wo, cache, post):
+    R, D = act.shape
+    n = 4
+    B = R // CHIPS
+    c = lax.axis_index("seq") // CORES
+    t, half, core, zz, i = jnp.meshgrid(*[jnp.arange(x, dtype=jnp.int32) for x in (PHASES, 2, 2, 2, B)], indexing="ij")
+    positions = TOK_DEV * (2 * t + core) + R * (2 * half + zz) + B * c + i
+    cosine, sine = rope_tables(positions.reshape(-1).astype(jnp.float32))
+    cosine = cosine.reshape(PHASES, 2, 4 * B, HD)
+    sine = sine.reshape(PHASES, 2, 4 * B, HD)
+    bf, f32 = jnp.bfloat16, jnp.float32
+    vmem = pl.BlockSpec(memory_space=pltpu.VMEM)
+    hbm = pl.BlockSpec(memory_space=pl.ANY)
+    dma = pltpu.SemaphoreType.DMA
+    KW, QW = wk.shape[1] // CORES, wq.shape[1] // CORES
+    cache = cache.reshape(2, 4, 2, CHIPS, B, wk.shape[1])
+    return pl.pallas_call(
+        phased_kernel,
+        out_shape=jax.ShapeDtypeStruct((R, D), bf),
+        in_specs=[vmem, vmem, hbm, hbm, hbm, hbm, hbm, vmem, vmem, vmem],
+        out_specs=vmem,
+        scratch_shapes=[
+            pltpu.VMEM((D, 2 * KW + QW), bf),
+            pltpu.VMEM(wo.shape, bf),
+            pltpu.VMEM((PHASES, B, D), bf),
+            pltpu.VMEM((PHASES, 2, CORES, 2, B, D), bf),
+            pltpu.VMEM((PHASES, 2, CORES, 2 * B, QW), bf),
+            pltpu.VMEM((4 + 4 * PHASES, 2, CHIPS, B, 2 * KW), bf),
+            pltpu.VMEM((PHASES, 2, 2 * B, CORES * QW), bf),
+            pltpu.VMEM((PHASES, 2, 2 * B, QW), bf),
+            pltpu.VMEM((PHASES, n + 1, B, D), bf),
+            pltpu.VMEM((2, n, B, D), f32),
+            pltpu.VMEM((PHASES, B, D), bf),
+            dma((4,)),
+            dma((2,)),
+            dma((3,)),
+            dma((CHIPS,)),
+            dma((PHASES, 2, n)),
+            dma((PHASES, n)),
+            dma((PHASES, n)),
+            dma((PHASES, n)),
+            dma((PHASES, 2, CORES, 3)),
+            dma((PHASES, 2, CORES, 3)),
+            dma((PHASES,)),
+            dma((PHASES,)),
+            dma((PHASES, n)),
+            dma((PHASES, n + 1)),
+            dma((PHASES,)),
+            dma((CHIPS,)),
+        ],
+        compiler_params=pltpu.CompilerParams(
+            collective_id=1, has_side_effects=True, vmem_limit_bytes=62 * 1024 * 1024
+        ),
+    )(act, gain, wq, wk, wv, wo, cache, post, cosine, sine)
+
+
 def solution(mesh):
+    if mesh.shape["head"] == 4 and mesh.shape["seq"] == CHIPS * CORES:
+        body = phased_per_device
+    else:
+        body = functools.partial(per_device, mesh.shape["head"], mesh.shape["seq"])
     return jax.shard_map(
-        functools.partial(per_device, mesh.shape["head"], mesh.shape["seq"]),
+        body,
         mesh=mesh,
         in_specs=(
             P(("seq", "head"), None),

time: 226 us -> 214 us (0.947)
  the two profiles are of different devices: /device:TPU:20 before, /device:TPU:7 now
where the time goes in v1:
time: 214 us
  Pallas kernels  208 us (97%)
  other arithmetic  3.31 us (2%)
  local copies, waits for them, and re-layouts  2.81 us (1%)
    pallas_call x1, Pallas kernels, phased_per_device(): pl.pallas_call(phased_kernel, out_shape=jax.ShapeDtypeStruct((R, D), bf),...  208 us

profile of v1, /device:TPU:7, one launch (start us, length us, event | category | flops | bytes accessed | tf_op | source)
XLA Modules:
  0.0 213.7 jit_solution(8672130251040019429)
XLA Ops:
  0.0 0.1 broadcast_in_dim.30
  0.1 0.1 broadcast_in_dim.28
  0.2 0.1 broadcast_in_dim.25
  0.3 0.1 add_convert_fusion
  0.4 1.9 fusion
  2.3 1.3 pad_maximum_fusion
  3.6 207.5 %shard_map.82 = bf16[128,5376]{1,0:T(8,128)(2,1)} custom-call(bf16[128,5376]{1,0:T(8,128)(2,1)} %act_ref.1, f32[5376]{0:T(1024)} %gain_ref.1, bf16[5376,1024]{1,0:T(8,128)(2,1)} %wq_hbm.1, bf16[5376,512]{1,0:T(8,128)(2,1)} %wk_hbm.1, bf16[5376,512]{1,0:T(8,128)(2,1)} %wv_hbm.1, bf16[1024,5376]{1,0:T(8,128)(2,1)} %wo_hbm.1, ...), custom_call_target="tpu_custom_call" | custom-call | tf_op jit(solution)/shard_map/pallas_call | solution.py:819
  211.2 2.5 %copy.10 = bf16[128,5376]{1,0:T(8,128)(2,1)} copy(bf16[128,5376]{1,0:T(8,128)(2,1)} %shard_map.82) | data formatting | bytes 2752512
  (6 shorter events, 0.0 us)

commit v2 on v1

--- a/solution.py
+++ b/solution.py
@@ -534,9 +534,6 @@
                         r0 = (core * 2 + zz) * B
                         c0 = part * KW + h * HD
                         kv[4 + 2 * (2 * t + core) + half, zz, c, :, c0:c0 + HD] = v[r0:r0 + B]
-        for d in range(3):
-            for core in range(2):
-                kv_copy(t, half, core, 2 - d, c).start()
 
         def queries(i, carry):
             c0 = pl.multiple_of(i * 256, 256)
@@ -547,6 +544,11 @@
                     q_buf[t, half, core, :, pl.ds(pl.multiple_of(c0 + h * HD, HD), HD)] = v[core * 2 * B:(core + 1) * 2 * B]
             return carry
         lax.fori_loop(0, QW // 256, queries, 0)
+
+    def send_kv(t, half):
+        for d in range(3):
+            for core in range(2):
+                kv_copy(t, half, core, 2 - d, c).start()
 
     M = group * 2 * B
     row = lax.rem(lax.broadcasted_iota(jnp.int32, (M, 256), 0), 2 * B)
@@ -582,25 +584,24 @@
                 c0 = dst_c0 + (g * group + a) * HD
                 dst[t, half, :, pl.ds(pl.multiple_of(c0, HD), HD)] = o_sum[a * 2 * B:(a + 1) * 2 * B]
 
-    def attend_halves(t, core, dst, dst_c0):
-        def one(half, carry):
-            attend(t, core, half, dst, dst_c0)
-            return carry
-        lax.fori_loop(0, 2, one, 0)
-
-    def att_copy(t, core):
+    def att_copy(t, half, core):
         return remote(
-            att_x.at[t], att.at[t, :, :, pl.ds(pl.multiple_of(core * QW, QW), QW)],
-            att_send.at[t], att_recv.at[t], c, 1 - k, z,
+            att_x.at[t, half], att.at[t, half, :, pl.ds(pl.multiple_of(core * QW, QW), QW)],
+            att_send.at[t, half], att_recv.at[t, half], c, 1 - k, z,
         )
 
     TILE = 256
 
-    def project_out(t):
+    def attend_half(t, half):
+        attend(t, 1 - k, half, att_x, 0)
+        att_copy(t, half, k).start()
+        attend(t, k, half, att, k * QW)
+        att_copy(t, half, 1 - k).wait_recv()
+
         def one(i, carry):
             w0 = pl.multiple_of(i * TILE, TILE)
-            p = jnp.dot(att[t].reshape(n * B, CORES * QW), wo[:, pl.ds(w0, TILE)], preferred_element_type=f32)
-            acc[lax.rem(t, 2), :, :, pl.ds(w0, TILE)] = p.reshape(n, B, TILE)
+            p = jnp.dot(att[t, half], wo[:, pl.ds(w0, TILE)], preferred_element_type=f32)
+            acc[lax.rem(t, 3), pl.ds(2 * half, 2), :, pl.ds(w0, TILE)] = p.reshape(2, B, TILE)
             return carry
         lax.fori_loop(0, D // TILE, one, 0)
 
@@ -612,67 +613,75 @@
             return jnp.where(low, n - 2, 1)
         return z + 1 - 2 * lax.rem(z, 2)
 
-    def rs_copy(t, b):
-        up = b > z
-        to = jnp.where(up, z + 1, z - 1)
+    H = B // 2
+
+    def rs_copy(t, b, piece):
+        to = jnp.where(b > z, z + 1, z - 1)
         slot = jnp.where(b == z - 1, n, b)
-        return remote(slots.at[t, b], slots.at[t, slot], rs_send.at[t, b], rs_recv.at[t, slot], c, k, to)
-
-    def rs_wait(t, slot):
-        remote(slots.at[t, slot], slots.at[t, slot], rs_send.at[t, 0], rs_recv.at[t, slot], c, k, z).wait_recv()
-
-    WIDE = 768
+        part = pl.ds(piece * H, H)
+        return remote(
+            slots.at[t, b, part, :], slots.at[t, slot, part, :],
+            rs_send.at[t, b, piece], rs_recv.at[t, slot, piece], c, k, to,
+        )
+
+    def rs_wait(t, slot, piece):
+        where = slots.at[t, slot, pl.ds(piece * H, H), :]
+        remote(where, where, rs_send.at[t, 0, piece], rs_recv.at[t, slot, piece], c, k, z).wait_recv()
+
+    WIDE = 1792
 
     def relay(t, r, incoming):
         b = relay_block(r)
-        if incoming:
-            rs_wait(t, b)
-
-        def one(i, carry):
-            c0 = pl.multiple_of(i * WIDE, WIDE)
-            x = acc[lax.rem(t, 2), b, :, pl.ds(c0, WIDE)]
+        for piece in range(2):
+            part = pl.ds(piece * H, H)
             if incoming:
-                x = x + slots[t, b, :, pl.ds(c0, WIDE)].astype(f32)
-            slots[t, b, :, pl.ds(c0, WIDE)] = x.astype(bf)
-            return carry
-        lax.fori_loop(0, D // WIDE, one, 0)
-        rs_copy(t, b).start()
-
-    def out_copy(t):
+                rs_wait(t, b, piece)
+
+            def one(i, carry):
+                c0 = pl.multiple_of(i * WIDE, WIDE)
+                x = acc[lax.rem(t, 3), b, part, pl.ds(c0, WIDE)]
+                if incoming:
+                    x = x + slots[t, b, part, pl.ds(c0, WIDE)].astype(f32)
+                slots[t, b, part, pl.ds(c0, WIDE)] = x.astype(bf)
+                return carry
+            lax.fori_loop(0, D // WIDE, one, 0)
+            rs_copy(t, b, piece).start()
+
+    def out_copy(t, piece):
         return remote(
-            stage.at[t], out_ref.at[pl.ds(pl.multiple_of(c * B, B), B), :], out_send.at[t], out_recv.at[c], t, k, z,
+            stage.at[t, pl.ds(piece * H, H), :],
+            out_ref.at[pl.ds(pl.multiple_of(c * B + piece * H, H), H), :],
+            out_send.at[t, piece], out_recv.at[c, piece], t, k, z,
         )
 
     def finish(t):
-        @pl.when(z > 0)
-        def _():
-            rs_wait(t, z)
-
-        @pl.when(z < n - 1)
-        def _():
-            rs_wait(t, n)
-
-        def piece(i, carry):
-            r0 = pl.multiple_of(i * 16, 16)
-            x = acc[lax.rem(t, 2), z, pl.ds(r0, 16), :]
-            x = x + jnp.where(z > 0, slots[t, z, pl.ds(r0, 16), :].astype(f32), 0.0)
-            x = x + jnp.where(z < n - 1, slots[t, n, pl.ds(r0, 16), :].astype(f32), 0.0)
+        for piece in range(2):
+            @pl.when(z > 0)
+            def _():
+                rs_wait(t, z, piece)
+
+            @pl.when(z < n - 1)
+            def _():
+                rs_wait(t, n, piece)
+
+            part = pl.ds(piece * H, H)
+            x = acc[lax.rem(t, 3), z, part, :]
+            x = x + jnp.where(z > 0, slots[t, z, part, :].astype(f32), 0.0)
+            x = x + jnp.where(z < n - 1, slots[t, n, part, :].astype(f32), 0.0)
             y = x * lax.rsqrt(jnp.mean(x * x, axis=-1, keepdims=True) + EPSILON) * post_ref[...].reshape(1, D)
-            y = (act_in[t, pl.ds(r0, 16), :].astype(f32) + y).astype(bf)
+            y = (act_in[t, part, :].astype(f32) + y).astype(bf)
 
             @pl.when(t == c)
             def _():
-                out_ref[pl.ds(pl.multiple_of(c * B + r0, 16), 16), :] = y
+                out_ref[pl.ds(pl.multiple_of(c * B + piece * H, H), H), :] = y
 
             @pl.when(t != c)
             def _():
-                stage[t, pl.ds(r0, 16), :] = y
-            return carry
-        lax.fori_loop(0, B // 16, piece, 0)
-
-        @pl.when(t != c)
-        def _():
-            out_copy(t).start()
+                stage[t, part, :] = y
+
+            @pl.when(t != c)
+            def _():
+                out_copy(t, piece).start()
 
     def spread():
         for d in range(3):
@@ -683,45 +692,53 @@
         spread()
 
     act_in[c] = act_ref[pl.ds(pl.multiple_of(c * B, B), B), :]
-    normalize(0)
-    forward(0, z, True, True)
+    normalize(c)
+    forward(c, z, True, True)
 
     @pl.when(c != 0)
     def _():
         spread()
+        normalize(0)
+        forward(0, z, True, True)
 
     for x in cache_copies + weight_copies:
         x.wait()
+
+    def own_rows(t):
+        @pl.when(t != c)
+        def _():
+            normalize(t)
+            forward(t, z, True, True)
 
     def slot_step(t, carry):
         gathers = t < PHASES
         computes = (t >= 1) & (t <= PHASES)
-        sums = t >= 2
+        sums = (t >= 2) & inner
+
+        @pl.when(computes)
+        def _():
+            project(t - 1, 1 - near)
+            send_kv(t - 1, 1 - near)
 
         @pl.when(gathers)
         def _():
             hop(t, 1)
 
-        @pl.when(computes)
-        def _():
-            project(t - 1, 1 - near)
-
-        @pl.when(t + 1 < PHASES)
-        def _():
-            normalize(t + 1)
-            forward(t + 1, z, True, True)
+        @pl.when((t >= 1) & (t + 1 < PHASES) & inner)
+        def _():
+            own_rows(t + 1)
 
         @pl.when(gathers)
         def _():
             project(t, near)
 
-        @pl.when(sums & inner)
+        @pl.when(t >= 3)
+        def _():
+            finish(t - 3)
+
+        @pl.when(sums)
         def _():
             relay(t - 2, 0, True)
-
-        @pl.when(gathers)
-        def _():
-            hop(t, 2)
 
         @pl.when(computes)
         def _():
@@ -729,31 +746,48 @@
                 for core in range(2):
                     for d in range(3):
                         kv_copy(t - 1, half, core, d, chip_at(d)).wait_recv()
-            attend_halves(t - 1, 1 - k, att_x, 0)
-            att_copy(t - 1, k).start()
-
-        @pl.when(sums & inner)
+
+        @pl.when(gathers)
+        def _():
+            send_kv(t, near)
+
+        @pl.when(t == 0)
+        def _():
+            def early(q, carry):
+                @pl.when(outer | (q == 1))
+                def _():
+                    own_rows(q)
+                return carry
+            lax.fori_loop(1, PHASES, early, 0)
+
+        @pl.when(computes)
+        def _():
+            attend_half(t - 1, 1 - near)
+
+            @pl.when(outer)
+            def _():
+                for r in range(2):
+                    relay(t - 1, r, False)
+
+        @pl.when(gathers)
+        def _():
+            hop(t, 2)
+
+        @pl.when(sums)
         def _():
             relay(t - 2, 1, True)
 
         @pl.when(computes)
         def _():
-            attend_halves(t - 1, k, att, k * QW)
-            att_copy(t - 1, 1 - k).wait_recv()
-            project_out(t - 1)
+            attend_half(t - 1, near)
 
             @pl.when(outer)
             def _():
-                for r in range(3):
-                    relay(t - 1, r, False)
-
-        @pl.when(sums & inner)
+                relay(t - 1, 2, False)
+
+        @pl.when(sums)
         def _():
             relay(t - 2, 2, True)
-
-        @pl.when(sums)
-        def _():
-            finish(t - 2)
 
         @pl.when(gathers)
         def _():
@@ -761,11 +795,13 @@
         return carry
 
     lax.fori_loop(0, PHASES + 2, slot_step, 0)
+    finish(PHASES - 1)
 
     for d in range(3):
         chip = chip_at(d)
-        where = out_ref.at[pl.ds(pl.multiple_of(chip * B, B), B), :]
-        remote(where, where, out_send.at[0], out_recv.at[chip], c, k, z).wait_recv()
+        for piece in range(2):
+            where = out_ref.at[pl.ds(pl.multiple_of(chip * B + piece * H, H), H), :]
+            remote(where, where, out_send.at[0, piece], out_recv.at[chip, piece], c, k, z).wait_recv()
 
     for d in range(3):
         spread_copy(d).wait_send()
@@ -784,18 +820,21 @@
 
             @pl.when(b != z)
             def _():
-                rs_copy(t, b).wait_send()
+                for piece in range(2):
+                    rs_copy(t, b, piece).wait_send()
             return carry
         lax.fori_loop(0, n, blocks, 0)
         for half in range(2):
             for core in range(2):
                 for d in range(3):
                     kv_copy(t, half, core, d, c).wait_send()
-        att_copy(t, k).wait_send()
+        for half in range(2):
+            att_copy(t, half, k).wait_send()
 
         @pl.when(t != c)
         def _():
-            out_copy(t).wait_send()
+            for piece in range(2):
+                out_copy(t, piece).wait_send()
         return carry
     lax.fori_loop(0, PHASES, drain, 0)
 
@@ -831,7 +870,7 @@
             pltpu.VMEM((PHASES, 2, 2 * B, CORES * QW), bf),
             pltpu.VMEM((PHASES, 2, 2 * B, QW), bf),
             pltpu.VMEM((PHASES, n + 1, B, D), bf),
-            pltpu.VMEM((2, n, B, D), f32),
+            pltpu.VMEM((3, n, B, D), f32),
             pltpu.VMEM((PHASES, B, D), bf),
             dma((4,)),
             dma((2,)),
@@ -843,12 +882,12 @@
             dma((PHASES, n)),
             dma((PHASES, 2, CORES, 3)),
             dma((PHASES, 2, CORES, 3)),
-            dma((PHASES,)),
-            dma((PHASES,)),
-            dma((PHASES, n)),
-            dma((PHASES, n + 1)),
-            dma((PHASES,)),
-            dma((CHIPS,)),
+            dma((PHASES, 2)),
+            dma((PHASES, 2)),
+            dma((PHASES, n, 2)),
+            dma((PHASES, n + 1, 2)),
+            dma((PHASES, 2)),
+            dma((CHIPS, 2)),
         ],
         compiler_params=pltpu.CompilerParams(
             collective_id=1, has_side_effects=True, vmem_limit_bytes=62 * 1024 * 1024

time: 214 us -> 193 us (0.902)
  Pallas kernels: 208 us -> 186 us
    pallas_call x1, Pallas kernels: 208 us -> 186 us  [phased_per_device(): pl.pallas_call(phased_kernel, out_shape=jax.ShapeDtypeStruct((R, D), bf),...]
where the time goes in v2:
time: 193 us; the launch traced here: 192 us
  Pallas kernels  186 us (96%)
  other arithmetic  3.31 us (2%)
  local copies, waits for them, and re-layouts  2.81 us (1%)
    pallas_call x1, Pallas kernels, phased_per_device(): pl.pallas_call(phased_kernel, out_shape=jax.ShapeDtypeStruct((R, D), bf),...  186 us

profile of v2, /device:TPU:7, one launch (start us, length us, event | category | flops | bytes accessed | tf_op | source)
XLA Modules:
  0.0 191.7 jit_solution(14429457036669153455)
XLA Ops:
  0.0 0.1 broadcast_in_dim.30
  0.1 0.1 broadcast_in_dim.28
  0.2 0.1 broadcast_in_dim.25
  0.3 0.1 add_convert_fusion
  0.4 1.9 fusion
  2.3 1.3 pad_maximum_fusion
  3.6 185.5 %shard_map.82 = bf16[128,5376]{1,0:T(8,128)(2,1)} custom-call(bf16[128,5376]{1,0:T(8,128)(2,1)} %act_ref.1, f32[5376]{0:T(1024)} %gain_ref.1, bf16[5376,1024]{1,0:T(8,128)(2,1)} %wq_hbm.1, bf16[5376,512]{1,0:T(8,128)(2,1)} %wk_hbm.1, bf16[5376,512]{1,0:T(8,128)(2,1)} %wv_hbm.1, bf16[1024,5376]{1,0:T(8,128)(2,1)} %wo_hbm.1, ...), custom_call_target="tpu_custom_call" | custom-call | tf_op jit(solution)/shard_map/pallas_call | solution.py:858
  189.2 2.5 %copy.10 = bf16[128,5376]{1,0:T(8,128)(2,1)} copy(bf16[128,5376]{1,0:T(8,128)(2,1)} %shard_map.82) | data formatting | bytes 2752512
  (6 shorter events, 0.0 us)

commit v3 on v2

--- a/solution.py
+++ b/solution.py
@@ -382,7 +382,7 @@
 
 
 def phased_kernel(
-    act_ref, gain_ref, wq_hbm, wk_hbm, wv_hbm, wo_hbm, cache_hbm, post_ref, cos_ref, sin_ref,
+    act_ref, gain_ref, wq_hbm, wk_hbm, wv_hbm, wo_hbm, cache_hbm, post_ref, far_cos, far_sin, low_cos, low_sin,
     out_ref,
     w, wo, act_in, rows, q_buf, kv, att, att_x, slots, acc, stage,
     w_sem, cache_sem, spread_send, spread_recv, ag_send, ag_recv, core_send, core_recv,
@@ -512,8 +512,15 @@
     def project(t, half):
         for i in range(2):
             core_copy(t, 2 * half + i, 1 - k).wait_recv()
-        cosine = cos_ref[t, half]
-        sine = sin_ref[t, half]
+        table = 4 * (2 * t + half)
+        cosine, sine = [], []
+        for i in range(4):
+            ca, sa = far_cos[table + i], far_sin[table + i]
+            cb, sb = low_cos[...], low_sin[...]
+            cosine.append(ca * cb - sa * sb)
+            sine.append(sa * cb + ca * sb)
+        cosine = jnp.concatenate(cosine, axis=0)
+        sine = jnp.concatenate(sine, axis=0)
         x = rows.at[t, half]
 
         def matmul(c0, width):
@@ -590,7 +597,7 @@
             att_send.at[t, half], att_recv.at[t, half], c, 1 - k, z,
         )
 
-    TILE = 256
+    TILE = 1792
 
     def attend_half(t, half):
         attend(t, 1 - k, half, att_x, 0)
@@ -751,6 +758,19 @@
         def _():
             send_kv(t, near)
 
+        @pl.when(computes)
+        def _():
+            attend_half(t - 1, 1 - near)
+
+            @pl.when(outer)
+            def _():
+                for r in range(2):
+                    relay(t - 1, r, False)
+
+        @pl.when(gathers)
+        def _():
+            hop(t, 2)
+
         @pl.when(t == 0)
         def _():
             def early(q, carry):
@@ -759,19 +779,6 @@
                     own_rows(q)
                 return carry
             lax.fori_loop(1, PHASES, early, 0)
-
-        @pl.when(computes)
-        def _():
-            attend_half(t - 1, 1 - near)
-
-            @pl.when(outer)
-            def _():
-                for r in range(2):
-                    relay(t - 1, r, False)
-
-        @pl.when(gathers)
-        def _():
-            hop(t, 2)
 
         @pl.when(sums)
         def _():
@@ -844,11 +851,13 @@
     n = 4
     B = R // CHIPS
     c = lax.axis_index("seq") // CORES
-    t, half, core, zz, i = jnp.meshgrid(*[jnp.arange(x, dtype=jnp.int32) for x in (PHASES, 2, 2, 2, B)], indexing="ij")
-    positions = TOK_DEV * (2 * t + core) + R * (2 * half + zz) + B * c + i
-    cosine, sine = rope_tables(positions.reshape(-1).astype(jnp.float32))
-    cosine = cosine.reshape(PHASES, 2, 4 * B, HD)
-    sine = sine.reshape(PHASES, 2, 4 * B, HD)
+    t, half, core, zz = jnp.meshgrid(*[jnp.arange(x, dtype=jnp.int32) for x in (PHASES, 2, 2, 2)], indexing="ij")
+    starts = TOK_DEV * (2 * t + core) + R * (2 * half + zz) + B * c
+    positions = jnp.concatenate([starts.reshape(-1), jnp.arange(B, dtype=jnp.int32)])
+    cosine, sine = rope_tables(positions.astype(jnp.float32))
+    blocks = starts.size
+    far = [x[:blocks].reshape(blocks, 1, HD) for x in (cosine, sine)]
+    low = [x[blocks:] for x in (cosine, sine)]
     bf, f32 = jnp.bfloat16, jnp.float32
     vmem = pl.BlockSpec(memory_space=pltpu.VMEM)
     hbm = pl.BlockSpec(memory_space=pl.ANY)
@@ -858,7 +867,7 @@
     return pl.pallas_call(
         phased_kernel,
         out_shape=jax.ShapeDtypeStruct((R, D), bf),
-        in_specs=[vmem, vmem, hbm, hbm, hbm, hbm, hbm, vmem, vmem, vmem],
+        in_specs=[vmem, vmem, hbm, hbm, hbm, hbm, hbm, vmem, vmem, vmem, vmem, vmem],
         out_specs=vmem,
         scratch_shapes=[
             pltpu.VMEM((D, 2 * KW + QW), bf),
@@ -892,7 +901,7 @@
         compiler_params=pltpu.CompilerParams(
             collective_id=1, has_side_effects=True, vmem_limit_bytes=62 * 1024 * 1024
         ),
-    )(act, gain, wq, wk, wv, wo, cache, post, cosine, sine)
+    )(act, gain, wq, wk, wv, wo, cache, post, *far, *low)
 
 
 def solution(mesh):

time: 193 us -> 176 us (0.912)
  Pallas kernels: 186 us -> 170 us
  other arithmetic: 3.31 us -> 1.08 us
    pallas_call x1, Pallas kernels: 186 us -> 170 us  [phased_per_device(): pl.pallas_call(phased_kernel, out_shape=jax.ShapeDtypeStruct((R, D), bf),...]
where the time goes in v3:
time: 176 us; the launch traced here: 174 us
  Pallas kernels  170 us (97%)
  local copies, waits for them, and re-layouts  2.6 us (1%)
    pallas_call x1, Pallas kernels, phased_per_device(): pl.pallas_call(phased_kernel, out_shape=jax.ShapeDtypeStruct((R, D), bf),...  170 us

profile of v3, /device:TPU:7, one launch (start us, length us, event | category | flops | bytes accessed | tf_op | source)
XLA Modules:
  0.0 173.8 jit_solution(3660948941179325148)
XLA Ops:
  0.0 0.1 add_add_fusion
  0.1 0.1 add.39
  0.2 0.1 add_convert_fusion
  0.3 0.2 multiply_sine_fusion
  0.5 0.7 pad_maximum_fusion
  1.2 170.1 %shard_map.82 = bf16[128,5376]{1,0:T(8,128)(2,1)} custom-call(bf16[128,5376]{1,0:T(8,128)(2,1)} %act_ref.1, f32[5376]{0:T(1024)} %gain_ref.1, bf16[5376,1024]{1,0:T(8,128)(2,1)} %wq_hbm.1, bf16[5376,512]{1,0:T(8,128)(2,1)} %wk_hbm.1, bf16[5376,512]{1,0:T(8,128)(2,1)} %wv_hbm.1, bf16[1024,5376]{1,0:T(8,128)(2,1)} %wo_hbm.1, ...), custom_call_target="tpu_custom_call" | custom-call | tf_op jit(solution)/shard_map/pallas_call | solution.py:867
  171.3 2.5 %copy.14 = bf16[128,5376]{1,0:T(8,128)(2,1)} copy(bf16[128,5376]{1,0:T(8,128)(2,1)} %shard_map.82) | data formatting | bytes 2752512
  (4 shorter events, 0.0 us)

commit v4 on v3

--- a/solution.py
+++ b/solution.py
@@ -386,7 +386,7 @@
     out_ref,
     w, wo, act_in, rows, q_buf, kv, att, att_x, slots, acc, stage,
     w_sem, cache_sem, spread_send, spread_recv, ag_send, ag_recv, core_send, core_recv,
-    kv_send, kv_recv, att_send, att_recv, rs_send, rs_recv, out_send, out_recv,
+    kv_send, kv_recv, att_send, att_recv, rs_send, rs_recv, out_send, out_recv, go_sem,
 ):
     n = 4
     s = lax.axis_index("seq")
@@ -458,17 +458,14 @@
     def spread_wait(t):
         remote(act_in.at[t], act_in.at[t], spread_send.at[0], spread_recv.at[t], c, k, z).wait_recv()
 
-    def row_block(t, core, zb):
-        return rows.at[t, zb // 2, core, lax.rem(zb, 2)]
-
     def ag_copy(t, direction, zb):
-        where = row_block(t, k, zb)
+        where = rows.at[2 * t + k, zb]
         to = jnp.minimum(z + 1, n - 1) if direction == 0 else jnp.maximum(z - 1, 0)
         return remote(where, where, ag_send.at[t, direction, zb], ag_recv.at[t, zb], c, k, to)
 
-    def core_copy(t, zb, core):
-        where = row_block(t, core, zb)
-        return remote(where, where, core_send.at[t, zb], core_recv.at[t, zb], c, 1 - k, z)
+    def core_copy(u, zb):
+        where = rows.at[u, zb]
+        return remote(where, where, core_send.at[u // 2, zb], core_recv.at[u // 2, zb], c, 1 - k, z)
 
     def normalize(t):
         @pl.when(t != c)
@@ -479,7 +476,7 @@
             r0 = pl.multiple_of(i * 16, 16)
             x = act_in[t, pl.ds(r0, 16), :].astype(f32)
             y = x * lax.rsqrt(jnp.mean(x * x, axis=-1, keepdims=True) + EPSILON) * gain_ref[...].reshape(1, D)
-            rows[t, near, k, lax.rem(z, 2), pl.ds(r0, 16), :] = y.astype(bf)
+            rows[2 * t + k, z, pl.ds(r0, 16), :] = y.astype(bf)
             return carry
         lax.fori_loop(0, B // 16, piece, 0)
 
@@ -492,7 +489,7 @@
             @pl.when(z > 0)
             def _():
                 ag_copy(t, 1, zb).start()
-        core_copy(t, zb, k).start()
+        core_copy(2 * t + k, zb).start()
 
     def hop(t, h):
         @pl.when(z - h >= 0)
@@ -505,57 +502,53 @@
             ag_copy(t, 1, z + h).wait_recv()
             forward(t, z + h, False, True)
 
-    def kv_copy(t, half, core, d, chip):
-        where = kv.at[4 + 2 * (2 * t + core) + half, :, chip]
-        return remote(where, where, kv_send.at[t, half, core, d], kv_recv.at[t, half, core, d], chip_at(d), k, z)
-
-    def project(t, half):
-        for i in range(2):
-            core_copy(t, 2 * half + i, 1 - k).wait_recv()
-        table = 4 * (2 * t + half)
+    def kv_copy(u, d, chip):
+        where = kv.at[pl.ds(4 + 2 * u, 2), :, chip]
+        return remote(where, where, kv_send.at[u, d], kv_recv.at[u, d], chip_at(d), k, z)
+
+    def project(u):
+        @pl.when(lax.rem(u, 2) != k)
+        def _():
+            for zb in range(n):
+                core_copy(u, zb).wait_recv()
+
         cosine, sine = [], []
-        for i in range(4):
-            ca, sa = far_cos[table + i], far_sin[table + i]
+        for i in range(n):
+            ca, sa = far_cos[4 * u + i], far_sin[4 * u + i]
             cb, sb = low_cos[...], low_sin[...]
             cosine.append(ca * cb - sa * sb)
             sine.append(sa * cb + ca * sb)
         cosine = jnp.concatenate(cosine, axis=0)
         sine = jnp.concatenate(sine, axis=0)
-        x = rows.at[t, half]
 
         def matmul(c0, width):
             return jnp.dot(
-                x[...].reshape(4 * B, D), w[:, pl.ds(c0, width)], preferred_element_type=f32
+                rows[u].reshape(n * B, D), w[:, pl.ds(c0, width)], preferred_element_type=f32
             )
 
-        def rope(u):
-            return u * cosine + pltpu.roll(u, HD // 2, 1) * sine
+        def rope(x):
+            return x * cosine + pltpu.roll(x, HD // 2, 1) * sine
 
         for part in range(2):
-            u = matmul(part * KW, KW)
+            x = matmul(part * KW, KW)
             for h in range(heads_kv):
-                v = u[:, h * HD:(h + 1) * HD]
+                v = x[:, h * HD:(h + 1) * HD]
                 v = (rope(v) if part == 0 else v).astype(bf)
-                for core in range(2):
-                    for zz in range(2):
-                        r0 = (core * 2 + zz) * B
-                        c0 = part * KW + h * HD
-                        kv[4 + 2 * (2 * t + core) + half, zz, c, :, c0:c0 + HD] = v[r0:r0 + B]
+                c0 = part * KW + h * HD
+                for zb in range(n):
+                    kv[4 + 2 * u + zb // 2, zb % 2, c, :, c0:c0 + HD] = v[zb * B:(zb + 1) * B]
+        for d in range(3):
+            kv_copy(u, 2 - d, c).start()
 
         def queries(i, carry):
             c0 = pl.multiple_of(i * 256, 256)
-            u = matmul(2 * KW + c0, 256)
+            x = matmul(2 * KW + c0, 256)
             for h in range(256 // HD):
-                v = (rope(u[:, h * HD:(h + 1) * HD]) * SCALAR ** (-0.5)).astype(bf)
-                for core in range(2):
-                    q_buf[t, half, core, :, pl.ds(pl.multiple_of(c0 + h * HD, HD), HD)] = v[core * 2 * B:(core + 1) * 2 * B]
+                v = (rope(x[:, h * HD:(h + 1) * HD]) * SCALAR ** (-0.5)).astype(bf)
+                for half in range(2):
+                    q_buf[u, half, :, pl.ds(pl.multiple_of(c0 + h * HD, HD), HD)] = v[half * 2 * B:(half + 1) * 2 * B]
             return carry
         lax.fori_loop(0, QW // 256, queries, 0)
-
-    def send_kv(t, half):
-        for d in range(3):
-            for core in range(2):
-                kv_copy(t, half, core, 2 - d, c).start()
 
     M = group * 2 * B
     row = lax.rem(lax.broadcasted_iota(jnp.int32, (M, 256), 0), 2 * B)
@@ -563,11 +556,12 @@
     later = lax.broadcasted_iota(jnp.int32, (M, 256), 1) > place
     spans = [(0, 1), (1, 3), (4, 1)]
 
-    def attend(t, core, half, dst, dst_c0):
-        u = 2 * (2 * t + core) + half
+    def attend(unit, half, dst, dst_c0):
+        t = unit // 2
+        u = 2 * unit + half
         for g in range(heads_kv):
             q = jnp.concatenate(
-                [q_buf[t, half, core, :, (g * group + a) * HD:(g * group + a + 1) * HD] for a in range(group)], axis=0
+                [q_buf[unit, half, :, (g * group + a) * HD:(g * group + a + 1) * HD] for a in range(group)], axis=0
             )
             scores = []
             for j, (o, wd) in enumerate(spans):
@@ -591,24 +585,25 @@
                 c0 = dst_c0 + (g * group + a) * HD
                 dst[t, half, :, pl.ds(pl.multiple_of(c0, HD), HD)] = o_sum[a * 2 * B:(a + 1) * 2 * B]
 
-    def att_copy(t, half, core):
+    def attend_halves(u, dst, dst_c0):
+        def one(half, carry):
+            attend(u, half, dst, dst_c0)
+            return carry
+        lax.fori_loop(0, 2, one, 0)
+
+    def att_copy(t, core):
         return remote(
-            att_x.at[t, half], att.at[t, half, :, pl.ds(pl.multiple_of(core * QW, QW), QW)],
-            att_send.at[t, half], att_recv.at[t, half], c, 1 - k, z,
+            att_x.at[t], att.at[t, :, :, pl.ds(pl.multiple_of(core * QW, QW), QW)],
+            att_send.at[t], att_recv.at[t], c, 1 - k, z,
         )
 
     TILE = 1792
 
-    def attend_half(t, half):
-        attend(t, 1 - k, half, att_x, 0)
-        att_copy(t, half, k).start()
-        attend(t, k, half, att, k * QW)
-        att_copy(t, half, 1 - k).wait_recv()
-
+    def project_out(t):
         def one(i, carry):
             w0 = pl.multiple_of(i * TILE, TILE)
-            p = jnp.dot(att[t, half], wo[:, pl.ds(w0, TILE)], preferred_element_type=f32)
-            acc[lax.rem(t, 3), pl.ds(2 * half, 2), :, pl.ds(w0, TILE)] = p.reshape(2, B, TILE)
+            p = jnp.dot(att[t].reshape(n * B, CORES * QW), wo[:, pl.ds(w0, TILE)], preferred_element_type=f32)
+            acc[lax.rem(t, 2), :, :, pl.ds(w0, TILE)] = p.reshape(n, B, TILE)
             return carry
         lax.fori_loop(0, D // TILE, one, 0)
 
@@ -646,7 +641,7 @@
 
             def one(i, carry):
                 c0 = pl.multiple_of(i * WIDE, WIDE)
-                x = acc[lax.rem(t, 3), b, part, pl.ds(c0, WIDE)]
+                x = acc[lax.rem(t, 2), b, part, pl.ds(c0, WIDE)]
                 if incoming:
                     x = x + slots[t, b, part, pl.ds(c0, WIDE)].astype(f32)
                 slots[t, b, part, pl.ds(c0, WIDE)] = x.astype(bf)
@@ -672,7 +667,7 @@
                 rs_wait(t, n, piece)
 
             part = pl.ds(piece * H, H)
-            x = acc[lax.rem(t, 3), z, part, :]
+            x = acc[lax.rem(t, 2), z, part, :]
             x = x + jnp.where(z > 0, slots[t, z, part, :].astype(f32), 0.0)
             x = x + jnp.where(z < n - 1, slots[t, n, part, :].astype(f32), 0.0)
             y = x * lax.rsqrt(jnp.mean(x * x, axis=-1, keepdims=True) + EPSILON) * post_ref[...].reshape(1, D)
@@ -694,7 +689,7 @@
         for d in range(3):
             spread_copy(2 - d).start()
 
-    @pl.when(c == 0)
+    @pl.when((c == 0) & (k == 0))
     def _():
         spread()
 
@@ -702,107 +697,111 @@
     normalize(c)
     forward(c, z, True, True)
 
+    @pl.when((c == 0) & (k == 0))
+    def _():
+        for d in range(3):
+            spread_copy(d).wait_send()
+        pl.semaphore_signal(go_sem, inc=1, device_id=(s + 1, z), device_id_type=MESH)
+
+    @pl.when((c == 0) & (k == 1))
+    def _():
+        pl.semaphore_wait(go_sem, 1)
+        spread()
+
     @pl.when(c != 0)
     def _():
+        @pl.when(k == 0)
+        def _():
+            normalize(0)
+            forward(0, z, True, True)
         spread()
-        normalize(0)
-        forward(0, z, True, True)
 
     for x in cache_copies + weight_copies:
         x.wait()
 
+    UNITS = PHASES * CORES
+
     def own_rows(t):
-        @pl.when(t != c)
+        @pl.when((t != c) & (t + k > 0))
         def _():
             normalize(t)
             forward(t, z, True, True)
 
-    def slot_step(t, carry):
-        gathers = t < PHASES
-        computes = (t >= 1) & (t <= PHASES)
-        sums = (t >= 2) & inner
-
-        @pl.when(computes)
-        def _():
-            project(t - 1, 1 - near)
-            send_kv(t - 1, 1 - near)
+    def step(j, carry):
+        mine = lax.rem(j, 2) == k
+        gathers = mine & (j < UNITS)
+        attends = (j >= 2) & (j <= UNITS + 1)
+        sums = (~mine) & inner & (j >= 3)
+        t = j // 2
+        behind = (j - 3) // 2
 
         @pl.when(gathers)
         def _():
             hop(t, 1)
 
-        @pl.when((t >= 1) & (t + 1 < PHASES) & inner)
-        def _():
-            own_rows(t + 1)
+        @pl.when((~mine) & (j + 1 < UNITS) & (inner | (j == 0)))
+        def _():
+            own_rows((j + 1) // 2)
+
+        @pl.when((j >= 1) & (j <= UNITS))
+        def _():
+            project(j - 1)
+
+        @pl.when(attends)
+        def _():
+            for d in range(3):
+                kv_copy(j - 2, d, chip_at(d)).wait_recv()
+
+            @pl.when(~mine)
+            def _():
+                attend_halves(j - 2, att_x, 0)
+                att_copy(t - 1, k).start()
+
+            @pl.when(mine)
+            def _():
+                attend_halves(j - 2, att, k * QW)
+                att_copy(t - 1, 1 - k).wait_recv()
+                project_out(t - 1)
+
+                @pl.when(outer)
+                def _():
+                    for r in range(3):
+                        relay(t - 1, r, False)
+
+        @pl.when(sums)
+        def _():
+            relay(behind, 0, True)
 
         @pl.when(gathers)
         def _():
-            project(t, near)
-
-        @pl.when(t >= 3)
-        def _():
-            finish(t - 3)
+            hop(t, 2)
+
+        @pl.when(outer & mine & (j <= 1))
+        def _():
+            lax.fori_loop(1, PHASES, lambda q, carry: (own_rows(q), carry)[1], 0)
 
         @pl.when(sums)
         def _():
-            relay(t - 2, 0, True)
-
-        @pl.when(computes)
-        def _():
-            for half in range(2):
-                for core in range(2):
-                    for d in range(3):
-                        kv_copy(t - 1, half, core, d, chip_at(d)).wait_recv()
+            relay(behind, 1, True)
+
+        @pl.when(mine & (j >= 4))
+        def _():
+            finish(t - 2)
 
         @pl.when(gathers)
         def _():
-            send_kv(t, near)
-
-        @pl.when(computes)
-        def _():
-            attend_half(t - 1, 1 - near)
-
-            @pl.when(outer)
-            def _():
-                for r in range(2):
-                    relay(t - 1, r, False)
-
-        @pl.when(gathers)
-        def _():
-            hop(t, 2)
-
-        @pl.when(t == 0)
-        def _():
-            def early(q, carry):
-                @pl.when(outer | (q == 1))
-                def _():
-                    own_rows(q)
-                return carry
-            lax.fori_loop(1, PHASES, early, 0)
+            hop(t, 3)
 
         @pl.when(sums)
         def _():
-            relay(t - 2, 1, True)
-
-        @pl.when(computes)
-        def _():
-            attend_half(t - 1, near)
-
-            @pl.when(outer)
-            def _():
-                relay(t - 1, 2, False)
-
-        @pl.when(sums)
-        def _():
-            relay(t - 2, 2, True)
-
-        @pl.when(gathers)
-        def _():
-            hop(t, 3)
+            relay(behind, 2, True)
         return carry
 
-    lax.fori_loop(0, PHASES + 2, slot_step, 0)
-    finish(PHASES - 1)
+    lax.fori_loop(0, UNITS + 3, step, 0)
+
+    @pl.when(k == 1)
+    def _():
+        finish(PHASES - 1)
 
     for d in range(3):
         chip = chip_at(d)
@@ -810,8 +809,10 @@
             where = out_ref.at[pl.ds(pl.multiple_of(chip * B + piece * H, H), H), :]
             remote(where, where, out_send.at[0, piece], out_recv.at[chip, piece], c, k, z).wait_recv()
 
-    for d in range(3):
-        spread_copy(d).wait_send()
+    @pl.when((c > 0) | (k > 0))
+    def _():
+        for d in range(3):
+            spread_copy(d).wait_send()
 
     def drain(t, carry):
         def blocks(b, carry):
@@ -823,7 +824,7 @@
             def _():
                 ag_copy(t, 1, b).wait_send()
 
-            core_copy(t, b, k).wait_send()
+            core_copy(2 * t + k, b).wait_send()
 
             @pl.when(b != z)
             def _():
@@ -831,12 +832,10 @@
                     rs_copy(t, b, piece).wait_send()
             return carry
         lax.fori_loop(0, n, blocks, 0)
-        for half in range(2):
-            for core in range(2):
-                for d in range(3):
-                    kv_copy(t, half, core, d, c).wait_send()
-        for half in range(2):
-            att_copy(t, half, k).wait_send()
+        for core in range(2):
+            for d in range(3):
+                kv_copy(2 * t + core, d, c).wait_send()
+        att_copy(t, k).wait_send()
 
         @pl.when(t != c)
         def _():
@@ -851,8 +850,7 @@
     n = 4
     B = R // CHIPS
     c = lax.axis_index("seq") // CORES
-    t, half, core, zz = jnp.meshgrid(*[jnp.arange(x, dtype=jnp.int32) for x in (PHASES, 2, 2, 2)], indexing="ij")
-    starts = TOK_DEV * (2 * t + core) + R * (2 * half + zz) + B * c
+    starts = R * jnp.arange(PHASES * CORES * n, dtype=jnp.int32) + B * c
     positions = jnp.concatenate([starts.reshape(-1), jnp.arange(B, dtype=jnp.int32)])
     cosine, sine = rope_tables(positions.astype(jnp.float32))
     blocks = starts.size
@@ -873,13 +871,13 @@
             pltpu.VMEM((D, 2 * KW + QW), bf),
             pltpu.VMEM(wo.shape, bf),
             pltpu.VMEM((PHASES, B, D), bf),
-            pltpu.VMEM((PHASES, 2, CORES, 2, B, D), bf),
-            pltpu.VMEM((PHASES, 2, CORES, 2 * B, QW), bf),
+            pltpu.VMEM((PHASES * CORES, n, B, D), bf),
+            pltpu.VMEM((PHASES * CORES, 2, 2 * B, QW), bf),
             pltpu.VMEM((4 + 4 * PHASES, 2, CHIPS, B, 2 * KW), bf),
             pltpu.VMEM((PHASES, 2, 2 * B, CORES * QW), bf),
             pltpu.VMEM((PHASES, 2, 2 * B, QW), bf),
             pltpu.VMEM((PHASES, n + 1, B, D), bf),
-            pltpu.VMEM((3, n, B, D), f32),
+            pltpu.VMEM((2, n, B, D), f32),
             pltpu.VMEM((PHASES, B, D), bf),
             dma((4,)),
             dma((2,)),
@@ -889,14 +887,15 @@
             dma((PHASES, n)),
             dma((PHASES, n)),
             dma((PHASES, n)),
-            dma((PHASES, 2, CORES, 3)),
-            dma((PHASES, 2, CORES, 3)),
-            dma((PHASES, 2)),
-            dma((PHASES, 2)),
+            dma((PHASES * CORES, 3)),
+            dma((PHASES * CORES, 3)),
+            dma((PHASES,)),
+            dma((PHASES,)),
             dma((PHASES, n, 2)),
             dma((PHASES, n + 1, 2)),
             dma((PHASES, 2)),
             dma((CHIPS, 2)),
+            pltpu.SemaphoreType.REGULAR,
         ],
         compiler_params=pltpu.CompilerParams(
             collective_id=1, has_side_effects=True, vmem_limit_bytes=62 * 1024 * 1024

time: 176 us -> 173 us (0.983); the launches traced: 174 us -> 173 us
  no operation moved by 1% of the time
where the time goes in v4:
time: 173 us
  Pallas kernels  169 us (98%)
  local copies, waits for them, and re-layouts  2.51 us (1%)
    pallas_call x1, Pallas kernels, phased_per_device(): pl.pallas_call(phased_kernel, out_shape=jax.ShapeDtypeStruct((R, D), bf),...  169 us

profile of v4, /device:TPU:7, one launch (start us, length us, event | category | flops | bytes accessed | tf_op | source)
XLA Modules:
  0.0 172.8 jit_solution(17728067877441411066)
XLA Ops:
  0.0 0.1 add_convert_fusion
  0.1 0.2 multiply_sine_fusion
  0.3 0.7 pad_maximum_fusion
  1.0 169.3 %shard_map.82 = bf16[128,5376]{1,0:T(8,128)(2,1)} custom-call(bf16[128,5376]{1,0:T(8,128)(2,1)} %act_ref.1, f32[5376]{0:T(1024)} %gain_ref.1, bf16[5376,1024]{1,0:T(8,128)(2,1)} %wq_hbm.1, bf16[5376,512]{1,0:T(8,128)(2,1)} %wk_hbm.1, bf16[5376,512]{1,0:T(8,128)(2,1)} %wv_hbm.1, bf16[1024,5376]{1,0:T(8,128)(2,1)} %wo_hbm.1, ...), custom_call_target="tpu_custom_call" | custom-call | tf_op jit(solution)/shard_map/pallas_call | solution.py:865
  170.3 2.5 %copy.12 = bf16[128,5376]{1,0:T(8,128)(2,1)} copy(bf16[128,5376]{1,0:T(8,128)(2,1)} %shard_map.82) | data formatting | bytes 2752512
  (3 shorter events, 0.0 us)

commit v5 on v4

--- a/solution.py
+++ b/solution.py
@@ -448,59 +448,65 @@
         x.start()
     pl.semaphore_wait(barrier, 4 + jnp.where(inner, 2, 1))
 
-    def spread_copy(d):
+    H = B // 2
+
+    def spread_copy(d, piece):
         to = chip_at(d)
         return remote(
-            act_ref.at[pl.ds(pl.multiple_of(to * B, B), B), :], act_in.at[c],
-            spread_send.at[d], spread_recv.at[c], to, k, z,
+            act_ref.at[pl.ds(pl.multiple_of(to * B + piece * H, H), H), :],
+            act_in.at[c, pl.ds(piece * H, H), :],
+            spread_send.at[d, piece], spread_recv.at[c, piece], to, k, z,
         )
 
-    def spread_wait(t):
-        remote(act_in.at[t], act_in.at[t], spread_send.at[0], spread_recv.at[t], c, k, z).wait_recv()
-
-    def ag_copy(t, direction, zb):
-        where = rows.at[2 * t + k, zb]
+    def spread_wait(t, piece):
+        where = act_in.at[t, pl.ds(piece * H, H), :]
+        remote(where, where, spread_send.at[0, piece], spread_recv.at[t, piece], c, k, z).wait_recv()
+
+    def ag_copy(t, direction, zb, piece):
+        where = rows.at[2 * t + k, zb, pl.ds(piece * H, H), :]
         to = jnp.minimum(z + 1, n - 1) if direction == 0 else jnp.maximum(z - 1, 0)
-        return remote(where, where, ag_send.at[t, direction, zb], ag_recv.at[t, zb], c, k, to)
-
-    def core_copy(u, zb):
-        where = rows.at[u, zb]
-        return remote(where, where, core_send.at[u // 2, zb], core_recv.at[u // 2, zb], c, 1 - k, z)
-
-    def normalize(t):
-        @pl.when(t != c)
-        def _():
-            spread_wait(t)
-
-        def piece(i, carry):
-            r0 = pl.multiple_of(i * 16, 16)
-            x = act_in[t, pl.ds(r0, 16), :].astype(f32)
-            y = x * lax.rsqrt(jnp.mean(x * x, axis=-1, keepdims=True) + EPSILON) * gain_ref[...].reshape(1, D)
-            rows[2 * t + k, z, pl.ds(r0, 16), :] = y.astype(bf)
-            return carry
-        lax.fori_loop(0, B // 16, piece, 0)
-
-    def forward(t, zb, right, left):
+        return remote(where, where, ag_send.at[t, direction, zb, piece], ag_recv.at[t, zb, piece], c, k, to)
+
+    def core_copy(u, zb, piece):
+        where = rows.at[u, zb, pl.ds(piece * H, H), :]
+        return remote(where, where, core_send.at[u // 2, zb, piece], core_recv.at[u // 2, zb, piece], c, 1 - k, z)
+
+    def forward(t, zb, right, left, piece):
         if right:
             @pl.when(z < n - 1)
             def _():
-                ag_copy(t, 0, zb).start()
+                ag_copy(t, 0, zb, piece).start()
         if left:
             @pl.when(z > 0)
             def _():
-                ag_copy(t, 1, zb).start()
-        core_copy(2 * t + k, zb).start()
+                ag_copy(t, 1, zb, piece).start()
+        core_copy(2 * t + k, zb, piece).start()
+
+    def normalize_and_send(t):
+        for piece in range(2):
+            part = pl.ds(piece * H, H)
+
+            @pl.when(t != c)
+            def _():
+                spread_wait(t, piece)
+
+            x = act_in[t, part, :].astype(f32)
+            y = x * lax.rsqrt(jnp.mean(x * x, axis=-1, keepdims=True) + EPSILON) * gain_ref[...].reshape(1, D)
+            rows[2 * t + k, z, part, :] = y.astype(bf)
+            forward(t, z, True, True, piece)
 
     def hop(t, h):
         @pl.when(z - h >= 0)
         def _():
-            ag_copy(t, 0, z - h).wait_recv()
-            forward(t, z - h, True, False)
+            for piece in range(2):
+                ag_copy(t, 0, z - h, piece).wait_recv()
+                forward(t, z - h, True, False, piece)
 
         @pl.when(z + h < n)
         def _():
-            ag_copy(t, 1, z + h).wait_recv()
-            forward(t, z + h, False, True)
+            for piece in range(2):
+                ag_copy(t, 1, z + h, piece).wait_recv()
+                forward(t, z + h, False, True, piece)
 
     def kv_copy(u, d, chip):
         where = kv.at[pl.ds(4 + 2 * u, 2), :, chip]
@@ -510,7 +516,8 @@
         @pl.when(lax.rem(u, 2) != k)
         def _():
             for zb in range(n):
-                core_copy(u, zb).wait_recv()
+                for piece in range(2):
+                    core_copy(u, zb, piece).wait_recv()
 
         cosine, sine = [], []
         for i in range(n):
@@ -615,8 +622,6 @@
             return jnp.where(low, n - 2, 1)
         return z + 1 - 2 * lax.rem(z, 2)
 
-    H = B // 2
-
     def rs_copy(t, b, piece):
         to = jnp.where(b > z, z + 1, z - 1)
         slot = jnp.where(b == z - 1, n, b)
@@ -686,21 +691,22 @@
                 out_copy(t, piece).start()
 
     def spread():
-        for d in range(3):
-            spread_copy(2 - d).start()
+        for piece in range(2):
+            for d in (2, 0, 1):
+                spread_copy(d, piece).start()
 
     @pl.when((c == 0) & (k == 0))
     def _():
         spread()
 
     act_in[c] = act_ref[pl.ds(pl.multiple_of(c * B, B), B), :]
-    normalize(c)
-    forward(c, z, True, True)
+    normalize_and_send(c)
 
     @pl.when((c == 0) & (k == 0))
     def _():
         for d in range(3):
-            spread_copy(d).wait_send()
+            for piece in range(2):
+                spread_copy(d, piece).wait_send()
         pl.semaphore_signal(go_sem, inc=1, device_id=(s + 1, z), device_id_type=MESH)
 
     @pl.when((c == 0) & (k == 1))
@@ -712,8 +718,7 @@
     def _():
         @pl.when(k == 0)
         def _():
-            normalize(0)
-            forward(0, z, True, True)
+            normalize_and_send(0)
         spread()
 
     for x in cache_copies + weight_copies:
@@ -724,8 +729,7 @@
     def own_rows(t):
         @pl.when((t != c) & (t + k > 0))
         def _():
-            normalize(t)
-            forward(t, z, True, True)
+            normalize_and_send(t)
 
     def step(j, carry):
         mine = lax.rem(j, 2) == k
@@ -812,19 +816,23 @@
     @pl.when((c > 0) | (k > 0))
     def _():
         for d in range(3):
-            spread_copy(d).wait_send()
+            for piece in range(2):
+                spread_copy(d, piece).wait_send()
 
     def drain(t, carry):
         def blocks(b, carry):
             @pl.when((b <= z) & (z < n - 1))
             def _():
-                ag_copy(t, 0, b).wait_send()
+                for piece in range(2):
+                    ag_copy(t, 0, b, piece).wait_send()
 
             @pl.when((b >= z) & (z > 0))
             def _():
-                ag_copy(t, 1, b).wait_send()
-
-            core_copy(2 * t + k, b).wait_send()
+                for piece in range(2):
+                    ag_copy(t, 1, b, piece).wait_send()
+
+            for piece in range(2):
+                core_copy(2 * t + k, b, piece).wait_send()
 
             @pl.when(b != z)
             def _():
@@ -881,12 +889,12 @@
             pltpu.VMEM((PHASES, B, D), bf),
             dma((4,)),
             dma((2,)),
-            dma((3,)),
-            dma((CHIPS,)),
-            dma((PHASES, 2, n)),
-            dma((PHASES, n)),
-            dma((PHASES, n)),
-            dma((PHASES, n)),
+            dma((3, 2)),
+            dma((CHIPS, 2)),
+            dma((PHASES, 2, n, 2)),
+            dma((PHASES, n, 2)),
+            dma((PHASES, n, 2)),
+            dma((PHASES, n, 2)),
             dma((PHASES * CORES, 3)),
             dma((PHASES * CORES, 3)),
             dma((PHASES,)),

time: 173 us -> 165 us (0.954)
  Pallas kernels: 169 us -> 161 us
    pallas_call x1, Pallas kernels: 169 us -> 161 us  [phased_per_device(): pl.pallas_call(phased_kernel, out_shape=jax.ShapeDtypeStruct((R, D), bf),...]
where the time goes in v5:
time: 165 us
  Pallas kernels  161 us (98%)
  local copies, waits for them, and re-layouts  2.51 us (2%)
    pallas_call x1, Pallas kernels, phased_per_device(): pl.pallas_call(phased_kernel, out_shape=jax.ShapeDtypeStruct((R, D), bf),...  161 us

profile of v5, /device:TPU:7, one launch (start us, length us, event | category | flops | bytes accessed | tf_op | source)
XLA Modules:
  0.0 164.6 jit_solution(10907288345776583682)
XLA Ops:
  0.0 0.1 add_convert_fusion
  0.1 0.2 multiply_sine_fusion
  0.3 0.7 pad_maximum_fusion
  1.0 161.1 %shard_map.82 = bf16[128,5376]{1,0:T(8,128)(2,1)} custom-call(bf16[128,5376]{1,0:T(8,128)(2,1)} %act_ref.1, f32[5376]{0:T(1024)} %gain_ref.1, bf16[5376,1024]{1,0:T(8,128)(2,1)} %wq_hbm.1, bf16[5376,512]{1,0:T(8,128)(2,1)} %wk_hbm.1, bf16[5376,512]{1,0:T(8,128)(2,1)} %wv_hbm.1, bf16[1024,5376]{1,0:T(8,128)(2,1)} %wo_hbm.1, ...), custom_call_target="tpu_custom_call" | custom-call | tf_op jit(solution)/shard_map/pallas_call | solution.py:873
  162.1 2.5 %copy.12 = bf16[128,5376]{1,0:T(8,128)(2,1)} copy(bf16[128,5376]{1,0:T(8,128)(2,1)} %shard_map.82) | data formatting | bytes 2752512
  (3 shorter events, 0.0 us)
